TPU v7x, 256 devices: a whole 4x4x8 slice. The times are simulated.
256 devices in a mesh: pair: 32 (over x, y, core), virt: 8 (over z).
Axes of the slice: x: 4, y: 4, z: 8, core: 2. Of those that a mesh axis runs over, the one named last changes fastest.
Arguments:
- amplitudes: bfloat16 [256, 1024, 1024], P(('pair', 'virt')), may hold values from -6 to 6
- lambda_two: bfloat16 [256, 1024, 1024], P(('pair', 'virt')), may hold values from -6 to 6
- lambda_omega: bfloat16 [256, 1024, 1024], P(('pair', 'virt')), may hold values from -6 to 6
- dipole_virtual: bfloat16 [1024, 1024], replicated, may hold values from -0.1875 to 0.1875
- dipole_occupied: float32 [120], replicated, may hold values from -1 to 1
- pair_orbitals: int32 [256, 2], P(('pair', 'virt')), may hold values from 0 to 119
- occupied_spin: int32 [120], replicated, may hold values from 0 to 1
- virtual_spin: int32 [1024], replicated, may hold values from 0 to 1
Outputs:
- response_gram: float32 [256, 256], P(('pair', 'virt'))
All inputs are finite; a program needn't handle non-finite values.
Results may differ from a plain program's by a relative error of at most 0.0025.
Values may be sent and summed in bfloat16 or wider, within the bound.
A program may use at most 64 MiB of HBM per device.

v0:
```python
import jax
import jax.numpy as jnp
from jax import lax
from jax.sharding import PartitionSpec as P


def gram_block(left_tile, right_tile):
    count = left_tile.shape[0]
    return lax.dot_general(
        left_tile.reshape(count, -1),
        right_tile.reshape(count, -1),
        (((1,), (1,)), ((), ())),
        preferred_element_type=jnp.float32,
    )


def tile_layout(block, count_pair, count_virt):
    count = block.shape[0]
    width = block.shape[1]
    shaped = block.reshape(count, count_pair, width // count_pair, count_virt, width // count_virt)
    return shaped.transpose(0, 1, 3, 2, 4)


def on_device(
    amplitudes,
    lambda_two,
    lambda_omega,
    dipole_virtual,
    dipole_occupied,
    pair_orbitals,
    occupied_spin,
    virtual_spin,
):
    occupied_count = dipole_occupied.shape[0]
    width = amplitudes.shape[1]
    per_device = amplitudes.shape[0]
    orbital_range = lax.iota(jnp.int32, occupied_count)[None, :]
    first_onehot = pair_orbitals[:, 0:1] == orbital_range
    second_onehot = pair_orbitals[:, 1:2] == orbital_range
    pair_shift = jnp.sum(jnp.where(first_onehot, dipole_occupied[None, :], 0.0), axis=1) + jnp.sum(
        jnp.where(second_onehot, dipole_occupied[None, :], 0.0), axis=1
    )
    pair_spin = jnp.sum(jnp.where(first_onehot, occupied_spin[None, :], 0), axis=1) + jnp.sum(
        jnp.where(second_onehot, occupied_spin[None, :], 0), axis=1
    )
    virtual_sums = virtual_spin[:, None] + virtual_spin[None, :]
    allowed = virtual_sums[None, :, :] == pair_spin[:, None, None]
    first_side = jnp.einsum(
        "ac,pcb->pab", dipole_virtual, amplitudes, preferred_element_type=jnp.float32
    )
    second_side = jnp.einsum(
        "pac,bc->pab", amplitudes, dipole_virtual, preferred_element_type=jnp.float32
    )
    commutator = (
        first_side + second_side - pair_shift[:, None, None] * amplitudes.astype(jnp.float32)
    )
    commuted = jnp.where(allowed, commutator, jnp.float32(0.0)).astype(jnp.bfloat16)
    masked_amps = jnp.where(allowed, amplitudes, jnp.zeros_like(amplitudes))
    count_pair = lax.axis_size("pair")
    count_virt = lax.axis_size("virt")
    tiled_two = tile_layout(lambda_two, count_pair, count_virt)
    tiled_omega = tile_layout(lambda_omega, count_pair, count_virt)
    tiled_commuted = tile_layout(commuted, count_pair, count_virt)
    tiled_masked = tile_layout(masked_amps, count_pair, count_virt)
    received = (
        lax.all_to_all(
            lax.all_to_all(tiled_two, "pair", split_axis=1, concat_axis=0, tiled=True),
            "virt",
            split_axis=2,
            concat_axis=0,
            tiled=True,
        ),
        lax.all_to_all(
            lax.all_to_all(tiled_omega, "pair", split_axis=1, concat_axis=0, tiled=True),
            "virt",
            split_axis=2,
            concat_axis=0,
            tiled=True,
        ),
        lax.all_to_all(
            lax.all_to_all(tiled_commuted, "pair", split_axis=1, concat_axis=0, tiled=True),
            "virt",
            split_axis=2,
            concat_axis=0,
            tiled=True,
        ),
        lax.all_to_all(
            lax.all_to_all(tiled_masked, "pair", split_axis=1, concat_axis=0, tiled=True),
            "virt",
            split_axis=2,
            concat_axis=0,
            tiled=True,
        ),
    )
    partial_value = gram_block(received[0], received[2]) + gram_block(received[1], received[3])
    partial_value = partial_value.reshape(
        count_virt, count_pair, per_device, count_virt, count_pair, per_device
    )
    partial_value = partial_value.transpose(1, 0, 2, 4, 3, 5).reshape(
        count_virt * count_pair * per_device, -1
    )
    partial_value = partial_value / jnp.float32(width)
    return lax.psum_scatter(partial_value, ("pair", "virt"), scatter_dimension=0, tiled=True)


def solution(mesh):
    return jax.shard_map(
        on_device,
        mesh=mesh,
        in_specs=(
            P(("pair", "virt"), None, None),
            P(("pair", "virt"), None, None),
            P(("pair", "virt"), None, None),
            P(),
            P(),
            P(("pair", "virt"), None),
            P(),
            P(),
        ),
        out_specs=P(("pair", "virt"), None),
        check_vma=False,
    )
```

profile of v0, /device:TPU:1, one launch (start us, length us, event | category | flops | bytes accessed | tf_op | source)
XLA Modules:
  0.0 662.7 jit_solution(9650075295484600187)
XLA Ops:
  8.0 2.6 fusion.34
  13.2 3.9 copy.36
  17.1 6.0 fusion.15
  25.7 7.5 %fusion.2 = bf16[1,1024,1024]{1,2,0:T(8,128)(2,1)} fusion(f32[1024,1024]{1,0:T(8,128)} %fusion.15, bf16[1,1024,1024]{1,2,0:T(8,128)(2,1)} %copy.36, bf16[1024,1024]{1,0:T(8,128)(2,1)S(1)} %copy-done, bf16[1,1024,1024]{2,1,0:T(8,128)(2,1)} %param.8, f32[]{:T(128)S(6)} %add.42, s32[]{:T(128)S(6)} %add.40, s32[1024]{0:T(1024)S(1)} %copy-done.2), kind=kOutput, calls=%fused_computation.3 | convolution fusion | flops 2155872256 | bytes 12587016 | tf_op jit(solution)/shard_map/pac,bc->pab/dot_general | solution.py:51
  33.2 2.9 copy.37
  38.0 8.6 %all-to-all-start = ((bf16[1,32,8,32,128]{4,2,3,0,1:T(8,128)(2,1)}), bf16[1,32,8,32,128]{4,2,3,0,1:T(8,128)(2,1)S(1)}, u32[]{:S(2)}, u32[]{:S(2)}) async-start(bf16[1,32,8,32,128]{4,2,3,0,1:T(8,128)(2,1)} %bitcast.113), calls=%async_computation | async-start | bytes 4194304 | tf_op jit(solution)/shard_map/all_to_all | solution.py:81
  46.6 3.6 fusion.3
  50.2 3.9 copy.43
  54.2 3.6 copy.54
  57.7 17.2 %all-to-all-done = bf16[1,32,8,32,128]{4,2,3,0,1:T(8,128)(2,1)S(1)} async-done(((bf16[1,32,8,32,128]{4,2,3,0,1:T(8,128)(2,1)}), bf16[1,32,8,32,128]{4,2,3,0,1:T(8,128)(2,1)S(1)}, u32[]{:S(2)}, u32[]{:S(2)}) %all-to-all-start) | async-done | bytes 2097184 | tf_op jit(solution)/shard_map/all_to_all | solution.py:81
  74.9 5.2 all-to-all-start.4
  84.2 24.4 %all-to-all-done.4 = bf16[1,32,8,32,128]{4,2,3,0,1:T(8,128)(2,1)} async-done(((bf16[1,32,8,32,128]{4,2,3,0,1:T(8,128)(2,1)}), bf16[1,32,8,32,128]{4,2,3,0,1:T(8,128)(2,1)}, u32[]{:S(2)}, u32[]{:S(2)}) %all-to-all-start.4) | async-done | bytes 2097184 | tf_op jit(solution)/shard_map/all_to_all | solution.py:88
  108.6 5.2 all-to-all-start.6
  117.9 24.4 %all-to-all-done.6 = bf16[1,32,8,32,128]{4,3,2,0,1:T(8,128)(2,1)} async-done(((bf16[1,32,8,32,128]{4,3,2,0,1:T(8,128)(2,1)}), bf16[1,32,8,32,128]{4,3,2,0,1:T(8,128)(2,1)}, u32[]{:S(2)}, u32[]{:S(2)}) %all-to-all-start.6) | async-done | bytes 2097184 | tf_op jit(solution)/shard_map/all_to_all | solution.py:74
  142.2 5.2 all-to-all-start.2
  149.1 26.7 %all-to-all-done.2 = bf16[1,32,8,32,128]{4,3,2,0,1:T(8,128)(2,1)} async-done(((bf16[1,32,8,32,128]{4,3,2,0,1:T(8,128)(2,1)}), bf16[1,32,8,32,128]{4,3,2,0,1:T(8,128)(2,1)}, u32[]{:S(2)}, u32[]{:S(2)}) %all-to-all-start.2) | async-done | bytes 2097184 | tf_op jit(solution)/shard_map/all_to_all | solution.py:67
  175.9 8.2 %all-to-all-start.1 = ((bf16[32,1,8,32,128]{4,3,0,1,2:T(8,128)(2,1)}), bf16[32,1,8,32,128]{4,3,0,1,2:T(8,128)(2,1)S(1)}, u32[]{:S(2)}, u32[]{:S(2)}) async-start(bf16[32,1,8,32,128]{4,3,0,1,2:T(8,128)(2,1)} %copy.39), calls=%async_computation.1 | async-start | bytes 4194304 | tf_op jit(solution)/shard_map/all_to_all | solution.py:80
  184.0 3.3 copy.45
  187.4 45.0 %all-to-all-done.1 = bf16[32,1,8,32,128]{4,3,0,1,2:T(8,128)(2,1)S(1)} async-done(((bf16[32,1,8,32,128]{4,3,0,1,2:T(8,128)(2,1)}), bf16[32,1,8,32,128]{4,3,0,1,2:T(8,128)(2,1)S(1)}, u32[]{:S(2)}, u32[]{:S(2)}) %all-to-all-start.1) | async-done | bytes 2097184 | tf_op jit(solution)/shard_map/all_to_all | solution.py:80
  232.4 4.7 all-to-all-start.5
  237.1 3.4 copy.47
  240.5 45.4 %all-to-all-done.5 = bf16[32,1,8,32,128]{4,3,0,1,2:T(8,128)(2,1)} async-done(((bf16[32,1,8,32,128]{4,3,0,1,2:T(8,128)(2,1)}), bf16[32,1,8,32,128]{4,3,0,1,2:T(8,128)(2,1)}, u32[]{:S(2)}, u32[]{:S(2)}) %all-to-all-start.5) | async-done | bytes 2097184 | tf_op jit(solution)/shard_map/all_to_all | solution.py:87
  285.8 4.3 all-to-all-start.7
  290.2 3.4 copy.41
  293.6 45.0 %all-to-all-done.7 = bf16[32,1,8,32,128]{4,3,0,1,2:T(8,128)(2,1)} async-done(((bf16[32,1,8,32,128]{4,3,0,1,2:T(8,128)(2,1)}), bf16[32,1,8,32,128]{4,3,0,1,2:T(8,128)(2,1)}, u32[]{:S(2)}, u32[]{:S(2)}) %all-to-all-start.7) | async-done | bytes 2097184 | tf_op jit(solution)/shard_map/all_to_all | solution.py:73
  338.6 4.4 all-to-all-start.3
  343.0 3.4 fusion.4
  346.5 44.7 %all-to-all-done.3 = bf16[32,1,8,32,128]{4,3,0,1,2:T(8,128)(2,1)} async-done(((bf16[32,1,8,32,128]{4,3,0,1,2:T(8,128)(2,1)}), bf16[32,1,8,32,128]{4,3,0,1,2:T(8,128)(2,1)}, u32[]{:S(2)}, u32[]{:S(2)}) %all-to-all-start.3) | async-done | bytes 2097184 | tf_op jit(solution)/shard_map/all_to_all | solution.py:66
  391.2 2.8 fusion.27
  394.3 4.4 copy.48
  398.7 4.9 div.19
  403.6 251.1 %all-reduce.3.cloned.1.call-done = f32[256,256]{1,0:T(8,128)} async-done(((f32[256,256]{1,0:T(8,128)}), f32[256,256]{1,0:T(8,128)}) %all-reduce.3.cloned.1.call-update) | async-done | bytes 262160
  (18 shorter events, 17.4 us)
Async XLA Ops:
  6.5 10.6 %copy-start = (bf16[1024,1024]{1,0:T(8,128)(2,1)S(1)}, bf16[1024,1024]{1,0:T(8,128)(2,1)}, u32[]{:S(2)}) copy-start(bf16[1024,1024]{1,0:T(8,128)(2,1)} %param.11) | copy-start | bytes 6291460
  17.1 8.5 %copy-start.2 = (s32[1024]{0:T(1024)S(1)}, s32[1024]{0:T(1024)}, u32[]{:S(2)}) copy-start(s32[1024]{0:T(1024)} %param.15) | copy-start | bytes 12292
  38.0 36.9 %all-to-all-start = ((bf16[1,32,8,32,128]{4,2,3,0,1:T(8,128)(2,1)}), bf16[1,32,8,32,128]{4,2,3,0,1:T(8,128)(2,1)S(1)}, u32[]{:S(2)}, u32[]{:S(2)}) async-start(bf16[1,32,8,32,128]{4,2,3,0,1:T(8,128)(2,1)} %bitcast.113), calls=%async_computation | async-start | bytes 4194304 | tf_op jit(solution)/shard_map/all_to_all | solution.py:81
  74.9 33.6 %all-to-all-start.4 = ((bf16[1,32,8,32,128]{4,2,3,0,1:T(8,128)(2,1)}), bf16[1,32,8,32,128]{4,2,3,0,1:T(8,128)(2,1)}, u32[]{:S(2)}, u32[]{:S(2)}) async-start(bf16[1,32,8,32,128]{4,2,3,0,1:T(8,128)(2,1)} %bitcast.112), calls=%async_computation.4 | async-start | bytes 4194304 | tf_op jit(solution)/shard_map/all_to_all | solution.py:88
  108.6 33.7 %all-to-all-start.6 = ((bf16[1,32,8,32,128]{4,3,2,0,1:T(8,128)(2,1)}), bf16[1,32,8,32,128]{4,3,2,0,1:T(8,128)(2,1)}, u32[]{:S(2)}, u32[]{:S(2)}) async-start(bf16[1,32,8,32,128]{4,3,2,0,1:T(8,128)(2,1)} %copy.46), calls=%async_computation.6 | async-start | bytes 4194304 | tf_op jit(solution)/shard_map/all_to_all | solution.py:74
  142.2 33.6 %all-to-all-start.2 = ((bf16[1,32,8,32,128]{4,3,2,0,1:T(8,128)(2,1)}), bf16[1,32,8,32,128]{4,3,2,0,1:T(8,128)(2,1)}, u32[]{:S(2)}, u32[]{:S(2)}) async-start(bf16[1,32,8,32,128]{4,3,2,0,1:T(8,128)(2,1)} %copy.40), calls=%async_computation.2 | async-start | bytes 4194304 | tf_op jit(solution)/shard_map/all_to_all | solution.py:67
  175.9 56.5 %all-to-all-start.1 = ((bf16[32,1,8,32,128]{4,3,0,1,2:T(8,128)(2,1)}), bf16[32,1,8,32,128]{4,3,0,1,2:T(8,128)(2,1)S(1)}, u32[]{:S(2)}, u32[]{:S(2)}) async-start(bf16[32,1,8,32,128]{4,3,0,1,2:T(8,128)(2,1)} %copy.39), calls=%async_computation.1 | async-start | bytes 4194304 | tf_op jit(solution)/shard_map/all_to_all | solution.py:80
  232.4 53.4 %all-to-all-start.5 = ((bf16[32,1,8,32,128]{4,3,0,1,2:T(8,128)(2,1)}), bf16[32,1,8,32,128]{4,3,0,1,2:T(8,128)(2,1)}, u32[]{:S(2)}, u32[]{:S(2)}) async-start(bf16[32,1,8,32,128]{4,3,0,1,2:T(8,128)(2,1)} %copy.45), calls=%async_computation.5 | async-start | bytes 4194304 | tf_op jit(solution)/shard_map/all_to_all | solution.py:87
  285.8 52.8 %all-to-all-start.7 = ((bf16[32,1,8,32,128]{4,3,0,1,2:T(8,128)(2,1)}), bf16[32,1,8,32,128]{4,3,0,1,2:T(8,128)(2,1)}, u32[]{:S(2)}, u32[]{:S(2)}) async-start(bf16[32,1,8,32,128]{4,3,0,1,2:T(8,128)(2,1)} %copy.47), calls=%async_computation.7 | async-start | bytes 4194304 | tf_op jit(solution)/shard_map/all_to_all | solution.py:73
  338.6 52.6 %all-to-all-start.3 = ((bf16[32,1,8,32,128]{4,3,0,1,2:T(8,128)(2,1)}), bf16[32,1,8,32,128]{4,3,0,1,2:T(8,128)(2,1)}, u32[]{:S(2)}, u32[]{:S(2)}) async-start(bf16[32,1,8,32,128]{4,3,0,1,2:T(8,128)(2,1)} %copy.41), calls=%async_computation.3 | async-start | bytes 4194304 | tf_op jit(solution)/shard_map/all_to_all | solution.py:66
  343.0 311.6 %all-reduce.3.cloned.1.call-start = ((), (), s32[]{:S(2)}) async-start(), calls=%async_computation.8 | async-start | bytes 524288
  398.7 257.2 %copy-start.1 = (bf16[1024,1024]{1,0:T(8,128)(2,1)S(1)}, bf16[1024,1024]{1,0:T(8,128)(2,1)}, u32[]{:S(2)}) copy-start(bf16[1024,1024]{1,0:T(8,128)(2,1)} %param.11) | copy-start | bytes 6291460
Sparse Core Ops, SparseCore 0:
  403.7 250.8 all-reduce.2
where the time goes:
time: 665 us; the launch traced here: 663 us
  waiting for transfers between devices  524 us (79%)
  local copies, waits for them, and re-layouts  48.4 us (7%)
  starting transfers between devices  45.8 us (7%)
  matrix products  19.8 us (3%)
  between operations  16 us (2%)
  other arithmetic  8.81 us (1%)
    unnamed x2, waiting for transfers between devices  251 us
    all_to_all x1, waiting for transfers between devices, on_device(): lax.all_to_all(lax.all_to_all(tiled_masked, 'pair', split_axis=1, concat_...  45.4 us
    all_to_all x1, waiting for transfers between devices, on_device(): lax.all_to_all(lax.all_to_all(tiled_omega, 'pair', split_axis=1, concat_a...  45 us
    all_to_all x1, waiting for transfers between devices, on_device(): lax.all_to_all(lax.all_to_all(tiled_commuted, 'pair', split_axis=1, conca...  45 us
    all_to_all x1, waiting for transfers between devices, on_device(): lax.all_to_all(lax.all_to_all(tiled_two, 'pair', split_axis=1, concat_axi...  44.7 us
    all_to_all x1, waiting for transfers between devices, on_device(): lax.all_to_all(tiled_two, 'pair', split_axis=1, concat_axis=0, tiled=True)  26.7 us
    all_to_all x1, waiting for transfers between devices, on_device(): lax.all_to_all(tiled_masked, 'pair', split_axis=1, concat_axis=0, tiled=T...  24.4 us
    all_to_all x1, waiting for transfers between devices, on_device(): lax.all_to_all(tiled_omega, 'pair', split_axis=1, concat_axis=0, tiled=True)  24.4 us
  transfers between devices with their start and end apart: 9, of which 9 were waited for; matrix products, arithmetic and copies ran while one was open for 5% of the time, Pallas kernels for 0%

commit v1 on v0

v1 whole, which is shorter than its diff:
```python
import functools

import jax
import jax.numpy as jnp
from jax import lax
from jax.experimental import pallas as pl
from jax.experimental.pallas import tpu as pltpu
from jax.sharding import PartitionSpec as P

MESH = pl.DeviceIdType.MESH
ROWS, LANES = 16, 256
BLOCK = 128
GROUP = 16


def kernel(
    count_pair,
    count_virt,
    amps_hbm,
    two_hbm,
    omega_hbm,
    dipole_hbm,
    occ_ref,
    orb_ref,
    ospin_ref,
    vspin_ref,
    out_ref,
    amps,
    dipole,
    commuted,
    masked,
    got_two,
    got_omega,
    got_commuted,
    got_masked,
    left,
    right,
    partial_sum,
    got_plane,
    slab,
    got_line,
    load_sem,
    own_sem,
    send_sem,
    recv_sem,
    plane_send,
    plane_recv,
    line_send,
    line_recv,
):
    pair = lax.axis_index("pair")
    virt = lax.axis_index("virt")
    me = pair * count_virt + virt
    count = count_pair * count_virt
    width = amps.shape[0]
    across = width // LANES

    load_amps = pltpu.make_async_copy(amps_hbm, amps, load_sem.at[0])
    load_dipole = pltpu.make_async_copy(dipole_hbm, dipole, load_sem.at[1])
    load_amps.start()
    load_dipole.start()

    def partner(step):
        return lax.rem(pair + step // count_virt, count_pair), lax.rem(virt + step, count_virt)

    barrier = pltpu.get_barrier_semaphore()

    @pl.loop(1, count)
    def _(step):
        pl.semaphore_signal(barrier, inc=1, device_id=partner(step), device_id_type=MESH)

    pl.semaphore_wait(barrier, count - 1)

    def tile(ref, owner):
        row = pl.multiple_of((owner // across) * ROWS, ROWS)
        col = pl.multiple_of((owner % across) * LANES, LANES)
        return ref.at[pl.ds(row, ROWS), pl.ds(col, LANES)]

    def slot(ref, owner):
        return ref.at[pl.ds(pl.multiple_of(owner * ROWS, ROWS), ROWS)]

    def send(which, source, target):
        pltpu.make_async_copy(tile(source, me), slot(target, me), own_sem.at[which]).start()

        @pl.loop(1, count)
        def _(step):
            to_pair, to_virt = partner(step)
            pltpu.make_async_remote_copy(
                src_ref=tile(source, to_pair * count_virt + to_virt),
                dst_ref=slot(target, me),
                send_sem=send_sem.at[which],
                recv_sem=recv_sem.at[which],
                device_id=(to_pair, to_virt),
                device_id_type=MESH,
            ).start()

    def all_of(which, target):
        rest = target.at[pl.ds(0, (count - 1) * ROWS)]
        return pltpu.make_async_remote_copy(
            src_ref=rest,
            dst_ref=rest,
            send_sem=send_sem.at[which],
            recv_sem=recv_sem.at[which],
            device_id=(pair, virt),
            device_id_type=MESH,
        )

    def arrived(which, source, target):
        pltpu.make_async_copy(tile(source, me), slot(target, me), own_sem.at[which]).wait()
        all_of(which, target).wait_recv()

    send(0, omega_hbm, got_omega)

    load_amps.wait()
    load_dipole.wait()
    first, second = orb_ref[0, 0], orb_ref[0, 1]
    shift = occ_ref[first] + occ_ref[second]
    target_spin = (ospin_ref[first] + ospin_ref[second]).astype(jnp.float32)
    spins = vspin_ref[...].astype(jnp.float32)

    @pl.loop(0, width // BLOCK)
    def _(block):
        at = pl.ds(pl.multiple_of(block * BLOCK, BLOCK), BLOCK)
        own = vspin_ref[:, at].astype(jnp.float32)
        column = jnp.broadcast_to(own, (BLOCK, BLOCK)).T[:, 0:1]
        allowed = (column + spins) == target_spin
        rows = amps[at, :]
        value = jnp.dot(dipole[at, :], amps[...], preferred_element_type=jnp.float32)
        value += lax.dot_general(
            rows, dipole[...], (((1,), (1,)), ((), ())), preferred_element_type=jnp.float32
        )
        wide = rows.astype(jnp.float32)
        value -= shift * wide
        commuted[at, :] = jnp.where(allowed, value, 0.0).astype(jnp.bfloat16)
        masked[at, :] = jnp.where(allowed, wide, 0.0).astype(jnp.bfloat16)

    send(1, masked, got_masked)
    send(2, two_hbm, got_two)
    send(3, commuted, got_commuted)

    size = GROUP * ROWS
    row_id = lax.broadcasted_iota(jnp.int32, (size, size), 0)
    col_id = lax.broadcasted_iota(jnp.int32, (size, size), 1)
    swap = (col_id == (row_id % GROUP) * ROWS + row_id // GROUP).astype(jnp.bfloat16)

    def regroup(got, into):
        @pl.loop(0, count // GROUP)
        def _(g):
            block = got[pl.ds(pl.multiple_of(g * size, size), size), :]
            moved = jnp.dot(swap, block, preferred_element_type=jnp.float32)
            into[:, pl.ds(pl.multiple_of(g * GROUP, GROUP), GROUP), :] = moved.reshape(
                ROWS, GROUP, LANES
            ).astype(jnp.bfloat16)

    def gram(first_time):
        if first_time:
            partial_sum[...] = jnp.zeros_like(partial_sum)

        @pl.loop(0, ROWS)
        def _(r):
            partial_sum[...] += lax.dot_general(
                left[r], right[r], (((1,), (1,)), ((), ())), preferred_element_type=jnp.float32
            )

    arrived(0, omega_hbm, got_omega)
    regroup(got_omega, left)
    arrived(1, masked, got_masked)
    regroup(got_masked, right)
    gram(True)
    arrived(2, two_hbm, got_two)
    regroup(got_two, left)
    arrived(3, commuted, got_commuted)
    regroup(got_commuted, right)
    gram(False)
    partial_sum[...] = partial_sum[...] * (1.0 / width)

    def strip(ref, owner):
        return ref.at[pl.ds(pl.multiple_of(owner * count_virt, count_virt), count_virt)]

    @pl.loop(1, count_pair)
    def _(step):
        to_pair = lax.rem(pair + step, count_pair)
        pltpu.make_async_remote_copy(
            src_ref=strip(partial_sum, to_pair),
            dst_ref=strip(got_plane, pair),
            send_sem=plane_send,
            recv_sem=plane_recv,
            device_id=(to_pair, virt),
            device_id_type=MESH,
        ).start()

    strip(got_plane, pair)[...] = strip(partial_sum, pair)[...]
    rest = got_plane.at[pl.ds(0, (count_pair - 1) * count_virt)]
    plane = pltpu.make_async_remote_copy(
        src_ref=rest,
        dst_ref=rest,
        send_sem=plane_send,
        recv_sem=plane_recv,
        device_id=(pair, virt),
        device_id_type=MESH,
    )
    plane.wait_recv()
    slab[...] = jnp.sum(got_plane[...].reshape(count_pair, count_virt, count), axis=0)

    lines = []
    for step in range(1, count_virt):
        to_virt = lax.rem(virt + step, count_virt)
        lines.append(
            pltpu.make_async_remote_copy(
                src_ref=slab,
                dst_ref=got_line.at[virt],
                send_sem=line_send,
                recv_sem=line_recv,
                device_id=(pair, to_virt),
                device_id_type=MESH,
            )
        )
        lines[-1].start()
    got_line[virt] = slab[...]
    rest_line = got_line.at[pl.ds(0, count_virt - 1)]
    line = pltpu.make_async_remote_copy(
        src_ref=rest_line,
        dst_ref=rest_line,
        send_sem=line_send,
        recv_sem=line_recv,
        device_id=(pair, virt),
        device_id_type=MESH,
    )
    line.wait_recv()
    total = got_line[0, pl.ds(virt, 1), :]
    for v in range(1, count_virt):
        total += got_line[v, pl.ds(virt, 1), :]
    out_ref[...] = total
    for which, target in enumerate((got_omega, got_masked, got_two, got_commuted)):
        all_of(which, target).wait_send()
    plane.wait_send()
    line.wait_send()


def solution(mesh):
    count_pair, count_virt = mesh.shape["pair"], mesh.shape["virt"]
    count = count_pair * count_virt

    def on_device(amps, two, omega, dipole, occ, orbitals, ospin, vspin):
        width = dipole.shape[0]
        half, full = jnp.bfloat16, jnp.float32
        vmem, smem, dma = pltpu.VMEM, pltpu.SMEM, pltpu.SemaphoreType.DMA
        return pl.pallas_call(
            functools.partial(kernel, count_pair, count_virt),
            out_shape=jax.ShapeDtypeStruct((1, count), full),
            in_specs=[pl.BlockSpec(memory_space=pl.ANY)] * 4
            + [pl.BlockSpec(memory_space=smem)] * 3
            + [pl.BlockSpec(memory_space=vmem)],
            out_specs=pl.BlockSpec(memory_space=vmem),
            scratch_shapes=[vmem((width, width), half)] * 4
            + [vmem((count * ROWS, LANES), half)] * 4
            + [vmem((ROWS, count, LANES), half)] * 2
            + [
                vmem((count, count), full),
                vmem((count, count), full),
                vmem((count_virt, count), full),
                vmem((count_virt, count_virt, count), full),
                dma((2,)),
                dma((4,)),
                dma((4,)),
                dma((4,)),
                dma,
                dma,
                dma,
                dma,
            ],
            compiler_params=pltpu.CompilerParams(
                collective_id=0, has_side_effects=True, vmem_limit_bytes=48 * 2**20
            ),
            name="response_gram",
        )(
            amps.reshape(width, width),
            two.reshape(width, width),
            omega.reshape(width, width),
            dipole,
            occ,
            orbitals,
            ospin,
            vspin.reshape(1, width),
        )

    rows = P(("pair", "virt"))
    return jax.shard_map(
        on_device,
        mesh=mesh,
        in_specs=(rows, rows, rows, P(), P(), rows, P(), P()),
        out_specs=P(("pair", "virt"), None),
        check_vma=False,
    )
```

time: 665 us -> 226 us (0.34)
  waiting for transfers between devices: 524 us -> 0 us
  Pallas kernels: 0 us -> 220 us
  starting transfers between devices: 45.8 us -> 0 us
  local copies, waits for them, and re-layouts: 48.4 us -> 6.4 us
  matrix products: 19.8 us -> 0 us
  between operations: 16 us -> 0.02 us
  other arithmetic: 8.81 us -> 0 us
    all_to_all x8 -> x0, waiting for transfers between devices: 273 us -> none  [the longest x1 45.4 us: on_device(): lax.all_to_all(lax.all_to_all(tiled_masked, 'pair', split_axis=1, concat_...]
    unnamed x2 -> x0, waiting for transfers between devices: 251 us -> none
    pallas_call x0 -> x1, Pallas kernels: none -> 220 us  [on_device(): pl.pallas_call(functools.partial(kernel, count_pair, count_virt), out_sha...]
    all_to_all x8 -> x0, starting transfers between devices: 45.8 us -> none  [the longest x1 8.59 us: on_device(): lax.all_to_all(tiled_commuted, 'pair', split_axis=1, concat_axis=0, tiled...]
    dot_general x4 -> x0, matrix products: 19.8 us -> none  [the longest x1 7.54 us: on_device(): jnp.einsum('pac,bc->pab', amplitudes, dipole_virtual, preferred_element_t...]
    all_to_all x4 -> x0, local copies, waits for them, and re-layouts: 11.8 us -> none  [the longest x1 3.39 us: on_device(): lax.all_to_all(tiled_two, 'pair', split_axis=1, concat_axis=0, tiled=True)]
    div x3 -> x0, local copies, waits for them, and re-layouts: 9.5 us -> none  [on_device(): partial_value = partial_value / jnp.float32(width)]
    unnamed x12 -> x13, local copies, waits for them, and re-layouts: 15.1 us -> 6.4 us
  transfers between devices with their start and end apart: 9 -> 0, of which waited for: 9 -> 0; matrix products, arithmetic and copies ran while one was open for 5% -> 0% of each run, Pallas kernels for 0% -> 0%
where the time goes in v1:
time: 226 us
  Pallas kernels  220 us (97%)
  local copies, waits for them, and re-layouts  6.4 us (3%)
    pallas_call x1, Pallas kernels, on_device(): pl.pallas_call(functools.partial(kernel, count_pair, count_virt), out_sha...  220 us
    unnamed x13, local copies, waits for them, and re-layouts  6.4 us

profile of v1, /device:TPU:1, one launch (start us, length us, event | category | flops | bytes accessed | tf_op | source)
XLA Modules:
  0.0 226.1 jit_solution(63521998106699095)
XLA Ops:
  0.0 0.0 copy-start
  0.0 1.6 copy-done
  1.6 0.0 copy-start.1
  1.6 1.6 copy-done.1
  3.2 0.0 copy-start.2
  3.2 0.7 copy-done.2
  3.9 0.0 copy-start.3
  3.9 0.7 copy-done.3
  4.5 0.0 copy-start.4
  4.5 0.7 copy-done.4
  5.2 0.0 copy-start.5
  5.2 0.7 copy-done.5
  5.8 219.6 %response_gram.1 = f32[1,256]{1,0:T(1,128)S(1)} custom-call(bf16[1024,1024]{1,0:T(8,128)(2,1)S(1)} %bitcast.4, bf16[1024,1024]{1,0:T(8,128)(2,1)S(1)} %bitcast.5, bf16[1024,1024]{1,0:T(8,128)(2,1)} %bitcast.7, bf16[1024,1024]{1,0:T(8,128)(2,1)} %dipole_hbm.1, f32[120]{0:T(128)S(1)} %copy-done.3, s32[1,2]{1,0:T(1,128)S(1)} %copy-done.4, s32[120]{0:T(128)S(1)} %copy-done.5, ...), custom_call_target="tpu_custom_call" | custom-call | tf_op jit(solution)/shard_map/response_gram/pallas_call | solution.py:248
  225.5 0.6 copy.10
Async XLA Ops:
  0.0 1.6 copy-start
  1.6 1.6 copy-start.1
  3.2 0.7 copy-start.2
  3.9 0.7 copy-start.3
  4.5 0.7 copy-start.4
  5.2 0.7 copy-start.5

commit v2 on v1

v2 whole, which is shorter than its diff:
```python
import functools

import jax
import jax.numpy as jnp
from jax import lax
from jax.experimental import pallas as pl
from jax.experimental.pallas import tpu as pltpu
from jax.sharding import PartitionSpec as P

MESH = pl.DeviceIdType.MESH
HALF, FULL = jnp.bfloat16, jnp.float32
ROWS, LANES = 16, 128
TILE = 2 * ROWS
BLOCK = 128
GROUP = 16
NARROW = 4
LAST = (((1,), (1,)), ((), ()))


def kernel(
    rings,
    count_virt,
    spill,
    amps_hbm,
    two_hbm,
    omega_hbm,
    dipole_hbm,
    occ_hbm,
    orb_hbm,
    ospin_hbm,
    vspin_hbm,
    out_ref,
    amps,
    dipole,
    omega,
    two,
    place,
    commuted,
    masked,
    put_omega,
    put_two,
    put_fold,
    put_spill,
    got_omega,
    got_two,
    got_fold,
    got_spill,
    left,
    right_masked,
    right_commuted,
    turned_masked,
    turned_commuted,
    partial_sum,
    ordered,
    got_plane,
    slab,
    got_line,
    occ,
    orb,
    ospin,
    vspin,
    own_target,
    plane_target,
    row_target,
    line_target,
    targets,
    load_sem,
    own_sem,
    send_sem,
    recv_sem,
    stage_send,
    stage_recv,
):
    pair = lax.axis_index("pair")
    virt = lax.axis_index("virt")
    count_pair = 2 * rings
    count = count_pair * count_virt
    me = pair * count_virt + virt
    width = amps.shape[0]
    strips = width // TILE
    blocks = width // BLOCK
    per_block = strips // blocks
    middle = width // 2

    loads = [
        pltpu.make_async_copy(source, into, load_sem.at[k])
        for k, (source, into) in enumerate(
            (
                (vspin_hbm, vspin),
                (omega_hbm, omega),
                (amps_hbm, amps),
                (dipole_hbm, dipole),
                (two_hbm, two),
                (occ_hbm, occ),
                (orb_hbm, orb),
                (ospin_hbm, ospin),
            )
        )
    ]
    for load in loads:
        load.start()

    def strip_of(p, v):
        ring, core = p // 2, p % 2
        turned = (v + ring) % count_virt
        spot = (turned % 4) * 4 + core * 2 + turned // 4
        return spot * 2 + ring // 8, ring % 8

    def owner_of(strip, column):
        spot, ring = strip // 2, (strip % 2) * 8 + column
        turned = (spot % 2) * 4 + spot // 4
        return ring * 2 + (spot // 2) % 2, (turned + count_virt * 2 - ring) % count_virt

    my_strip, my_column = strip_of(pair, virt)
    spills = my_strip >= strips - spill

    def tile(ref, strip, column):
        row = pl.multiple_of(strip * TILE, TILE)
        col = pl.multiple_of(column * LANES, LANES)
        return ref.at[pl.ds(row, TILE), pl.ds(col, LANES)]

    def slot(ref, owner):
        return ref.at[pl.ds(pl.multiple_of(owner * TILE, TILE), TILE)]

    def push(which, source, target, strip, column, base, here, sem):
        p, v = owner_of(strip, column)
        mine = p * count_virt + v == me

        @pl.when(mine)
        def _():
            pltpu.make_async_copy(
                tile(source, strip - base, column), slot(target, here), own_sem.at[which]
            ).start()

        @pl.when(jnp.logical_not(mine))
        def _():
            pltpu.make_async_remote_copy(
                src_ref=tile(source, strip - base, column),
                dst_ref=slot(target, here),
                send_sem=send_sem.at[which],
                recv_sem=recv_sem.at[sem],
                device_id=(p, v),
                device_id_type=MESH,
            ).start()

    def send(which, make, source, target, here, sem):
        @pl.loop(0, blocks)
        def _(k):
            block = lax.rem(k + virt, blocks)
            make(block)

            @pl.loop(0, per_block * 8)
            def _(i):
                j = lax.rem(i + 2 * (pair // 2), per_block * 8)
                push(
                    which,
                    source,
                    target,
                    block * per_block + (j % 2) * 2 + (j // 2) % 2,
                    j // 4,
                    0,
                    here,
                    sem,
                )

    def waiter(which, sem, target, copies):
        part = target.at[pl.ds(0, copies * TILE)]
        return pltpu.make_async_remote_copy(
            src_ref=part,
            dst_ref=part,
            send_sem=send_sem.at[which],
            recv_sem=recv_sem.at[sem],
            device_id=(pair, virt),
            device_id_type=MESH,
        )

    def own_arrived(which, source, target, base, here):
        pltpu.make_async_copy(
            tile(source, my_strip - base, my_column), slot(target, here), own_sem.at[which]
        ).wait()

    loads[0].wait()
    spins = vspin[...].astype(FULL)
    before = (
        lax.broadcasted_iota(jnp.int32, (BLOCK, BLOCK), 0)
        < lax.broadcasted_iota(jnp.int32, (BLOCK, BLOCK), 1)
    ).astype(FULL)
    ones_before = jnp.dot(spins, before, preferred_element_type=FULL)
    ones = jnp.zeros((1, 1), FULL)
    lane = lax.broadcasted_iota(jnp.int32, (1, BLOCK), 1)
    new_row = lax.broadcasted_iota(jnp.int32, (width, BLOCK), 0)
    for k in range(blocks):
        spin = spins[k : k + 1, :]
        up = (ones_before[k : k + 1, :] + ones).astype(jnp.int32)
        spin_up = spin.astype(jnp.int32)
        rank = jnp.where(spin_up == 1, up, lane + k * BLOCK - up)
        inside = rank < middle
        row = jnp.where(inside, rank, width - 1 - rank)
        bottom = jnp.where(inside, spin_up, 1 - spin_up)
        goal = row + (row & -ROWS) + bottom * ROWS
        place[:, k * BLOCK : (k + 1) * BLOCK] = jnp.where(new_row == goal, 1.0, 0.0).astype(HALF)
        ones += jnp.sum(spin, axis=1, keepdims=True)
    zeros = width - ones

    def permuted(block, source):
        at = pl.ds(pl.multiple_of(block * BLOCK, BLOCK), BLOCK)
        return jnp.dot(place[at, :], source[...], preferred_element_type=FULL), at

    def make_from(source, put):
        def make(block):
            moved, at = permuted(block, source)
            put[at, :] = moved.astype(HALF)

        return make

    loads[1].wait()
    turned_me = virt * count_pair + pair
    send(0, make_from(omega, put_omega), put_omega, got_omega, turned_me, 0)

    for load in loads[2:]:
        load.wait()
    first, second = orb[0, 0], orb[0, 1]
    shift = occ[first] + occ[second]
    target_spin = (ospin[first] + ospin[second]).astype(FULL)
    all_spins = jnp.concatenate([spins[k : k + 1, :] for k in range(blocks)], axis=1)

    @pl.loop(0, blocks)
    def _(block):
        at = pl.ds(pl.multiple_of(block * BLOCK, BLOCK), BLOCK)
        own = vspin[pl.ds(block, 1), :].astype(FULL)
        column = jnp.broadcast_to(own, (BLOCK, BLOCK)).T[:, 0:1]
        allowed = (column + all_spins) == target_spin
        rows = amps[at, :]
        value = jnp.dot(dipole[at, :], amps[...], preferred_element_type=FULL)
        value += lax.dot_general(rows, dipole[...], LAST, preferred_element_type=FULL)
        wide = rows.astype(FULL)
        value -= shift * wide
        commuted[at, :] = jnp.where(allowed, value, 0.0).astype(HALF)
        masked[at, :] = jnp.where(allowed, wide, 0.0).astype(HALF)

    def make_fold(block):
        row = (
            (block * per_block + lax.broadcasted_iota(jnp.int32, (per_block, ROWS, 1), 0)) * ROWS
            + lax.broadcasted_iota(jnp.int32, (per_block, ROWS, 1), 1)
        ).astype(FULL)
        top_in = row < zeros[:, :, None]
        bottom_in = row < ones[:, :, None]
        kept, over = [], []
        for source in (commuted, masked):
            moved, at = permuted(block, source)
            moved = moved.reshape(per_block, 2, ROWS, width)
            top, bottom = moved[:, 0], moved[:, 1]
            kept.append(jnp.where(top_in, top, 0.0) + jnp.where(bottom_in, bottom, 0.0))
            over.append(jnp.where(top_in, 0.0, top) + jnp.where(bottom_in, 0.0, bottom))
        put_fold[at, :] = jnp.stack(kept, axis=1).reshape(BLOCK, width).astype(HALF)
        first_spill = (strips - spill) // per_block

        @pl.when(block >= first_spill)
        def _():
            to = pl.ds(pl.multiple_of((block - first_spill) * BLOCK, BLOCK), BLOCK)
            put_spill[to, :] = jnp.stack(over, axis=1).reshape(BLOCK, width).astype(HALF)

    send(1, make_fold, put_fold, got_fold, me, 1)

    owners = spill * 8

    @pl.loop(0, owners)
    def _(i):
        j = lax.rem(i + me, owners)
        push(
            2, put_spill, got_spill, strips - spill + j // 8, j % 8, strips - spill, me, 2
        )

    send(3, make_from(two, put_two), put_two, got_two, turned_me, 3 + virt)

    def stage(which, copies, ref):
        part = ref.at[pl.ds(0, copies)]
        return pltpu.make_async_remote_copy(
            src_ref=part,
            dst_ref=part,
            send_sem=stage_send.at[which],
            recv_sem=stage_recv.at[which],
            device_id=(pair, virt),
            device_id_type=MESH,
        )

    own_target[...] = jnp.full((1, LANES), 1.0, FULL) * target_spin
    plane_target[pair] = own_target[...]

    @pl.loop(1, count_pair)
    def _(step):
        pltpu.make_async_remote_copy(
            src_ref=own_target,
            dst_ref=plane_target.at[pair],
            send_sem=stage_send.at[0],
            recv_sem=stage_recv.at[0],
            device_id=(lax.rem(pair + step, count_pair), virt),
            device_id_type=MESH,
        ).start()

    stage(0, count_pair - 1, plane_target).wait_recv()
    gathered = jnp.zeros((1, LANES), FULL)
    for p in range(count_pair):
        gathered = jnp.where(lane == p, plane_target[p], gathered)
    row_target[...] = gathered
    line_target[virt] = gathered
    for step in range(1, count_virt):
        pltpu.make_async_remote_copy(
            src_ref=row_target,
            dst_ref=line_target.at[virt],
            send_sem=stage_send.at[1],
            recv_sem=stage_recv.at[1],
            device_id=(pair, lax.rem(virt + step, count_virt)),
            device_id_type=MESH,
        ).start()
    stage(1, count_virt - 1, line_target).wait_recv()
    for v in range(count_virt):
        column = jnp.broadcast_to(line_target[v], (LANES, LANES)).T
        targets[pl.ds(v, count_pair, stride=count_virt), :] = column[0:count_pair]
    my_spins = vspin[pl.ds(my_column, 1), :].astype(FULL)

    size = GROUP * ROWS
    row_id = lax.broadcasted_iota(jnp.int32, (size, size), 0)
    col_id = lax.broadcasted_iota(jnp.int32, (size, size), 1)
    swap = (col_id == (row_id % GROUP) * ROWS + row_id // GROUP).astype(HALF)

    def regrouped(got, g):
        block = got[pl.ds(pl.multiple_of(g * GROUP * TILE, GROUP * TILE), GROUP * TILE), :]
        block = block.reshape(GROUP, 2, ROWS, LANES)
        wide = jnp.concatenate(
            [block[:, 0].reshape(size, LANES), block[:, 1].reshape(size, LANES)], axis=1
        )
        moved = jnp.dot(swap, wide, preferred_element_type=FULL)
        return moved.reshape(ROWS, GROUP, 2 * LANES)

    def regroup(got, into, g):
        at = pl.ds(pl.multiple_of(g * GROUP, GROUP), GROUP)
        moved = regrouped(got, g).astype(HALF)
        for r in range(ROWS):
            into[at, r * 2 * LANES : (r + 1) * 2 * LANES] = moved[r]

    def unfold(with_spill):
        @pl.loop(0, count // GROUP)
        def _(g):
            at = pl.ds(pl.multiple_of(g * GROUP, GROUP), GROUP)
            target = targets[at, :]
            top = (target == my_spins)[None]
            bottom = (target == my_spins + 1.0)[None]
            main = regrouped(got_fold, g)
            over = regrouped(got_spill, g) if with_spill else None
            for k, into in enumerate((right_commuted, right_masked)):
                half = main[:, :, k * LANES : (k + 1) * LANES]
                rest = over[:, :, k * LANES : (k + 1) * LANES] if with_spill else 0.0
                upper = jnp.where(top, half, jnp.where(bottom, rest, 0.0)).astype(HALF)
                lower = jnp.where(bottom, half, jnp.where(top, rest, 0.0)).astype(HALF)
                for r in range(ROWS):
                    into[at, 2 * r * LANES : (2 * r + 1) * LANES] = upper[r]
                    into[at, (2 * r + 1) * LANES : (2 * r + 2) * LANES] = lower[r]

        @pl.loop(0, ROWS)
        def _(r):
            at = pl.ds(pl.multiple_of(r * 2 * LANES, 2 * LANES), 2 * LANES)
            for flat, turned in ((right_commuted, turned_commuted), (right_masked, turned_masked)):
                turned[at, :] = flat[:, at].T

    own_arrived(0, put_omega, got_omega, 0, turned_me)
    waiter(0, 0, got_omega, count - 1).wait_recv()

    @pl.loop(0, count // GROUP)
    def _(g):
        regroup(got_omega, left, g)

    own_arrived(1, put_fold, got_fold, 0, me)
    waiter(1, 1, got_fold, count - 1).wait_recv()

    @pl.when(spills)
    def _():
        own_arrived(2, put_spill, got_spill, strips - spill, me)
        waiter(2, 2, got_spill, count - 1).wait_recv()
        unfold(True)

    @pl.when(jnp.logical_not(spills))
    def _():
        unfold(False)

    partial_sum[...] = jnp.dot(left[...], turned_masked[...], preferred_element_type=FULL)
    my_block = my_strip // per_block

    @pl.loop(0, count_virt)
    def _(k):
        v = lax.rem(my_block + count_virt - k, count_virt)

        @pl.when(v == virt)
        def _():
            own_arrived(3, put_two, got_two, 0, turned_me)
            waiter(3, 3 + v, got_two, count_pair - 1).wait_recv()

        @pl.when(v != virt)
        def _():
            waiter(3, 3 + v, got_two, count_pair).wait_recv()

        for half in range(count_pair // GROUP):
            regroup(got_two, left, v * (count_pair // GROUP) + half)

    partial_sum[...] = (
        partial_sum[...] + jnp.dot(left[...], turned_commuted[...], preferred_element_type=FULL)
    ) * (1.0 / width)
    for v in range(count_virt):
        for h in range(count // LANES):
            ordered[h, pl.ds(v, count_pair, stride=count_virt), :] = partial_sum[
                v * count_pair : (v + 1) * count_pair, h * LANES : (h + 1) * LANES
            ]

    def rows_of(ref, owner):
        return ref.at[:, pl.ds(pl.multiple_of(owner * count_virt, count_virt), count_virt)]

    for step in range(1, count_pair):
        to_pair = lax.rem(pair + step, count_pair)
        pltpu.make_async_remote_copy(
            src_ref=rows_of(ordered, to_pair),
            dst_ref=rows_of(got_plane, pair),
            send_sem=stage_send.at[2],
            recv_sem=stage_recv.at[2],
            device_id=(to_pair, virt),
            device_id_type=MESH,
        ).start()

    rows_of(got_plane, pair)[...] = rows_of(ordered, pair)[...]
    rest = got_plane.at[:, pl.ds(0, (count_pair - 1) * count_virt)]
    plane = pltpu.make_async_remote_copy(
        src_ref=rest,
        dst_ref=rest,
        send_sem=stage_send.at[2],
        recv_sem=stage_recv.at[2],
        device_id=(pair, virt),
        device_id_type=MESH,
    )
    plane.wait_recv()
    slab[...] = jnp.sum(
        got_plane[...].reshape(count // LANES, count_pair, count_virt, LANES), axis=1
    )

    for step in range(1, count_virt):
        pltpu.make_async_remote_copy(
            src_ref=slab,
            dst_ref=got_line.at[virt],
            send_sem=stage_send.at[3],
            recv_sem=stage_recv.at[3],
            device_id=(pair, lax.rem(virt + step, count_virt)),
            device_id_type=MESH,
        ).start()
    got_line[virt] = slab[...]
    line = stage(3, count_virt - 1, got_line)
    line.wait_recv()
    for h in range(count // LANES):
        total = got_line[0, h, pl.ds(virt, 1), :]
        for v in range(1, count_virt):
            total += got_line[v, h, pl.ds(virt, 1), :]
        out_ref[:, h * LANES : (h + 1) * LANES] = total
    for which, target in ((0, got_omega), (1, got_fold), (3, got_two)):
        waiter(which, which, target, count - 1).wait_send()

    @pl.when(spills)
    def _():
        waiter(2, 2, got_spill, owners - 1).wait_send()

    @pl.when(jnp.logical_not(spills))
    def _():
        waiter(2, 2, got_spill, owners).wait_send()

    stage(0, count_pair - 1, plane_target).wait_send()
    stage(1, count_virt - 1, line_target).wait_send()
    plane.wait_send()
    line.wait_send()


def solution(mesh):
    count_pair, count_virt = mesh.shape["pair"], mesh.shape["virt"]
    count = count_pair * count_virt

    def on_device(amps, two, omega, dipole, occ, orbitals, ospin, vspin):
        width = dipole.shape[0]
        vmem, smem, dma = pltpu.VMEM, pltpu.SMEM, pltpu.SemaphoreType.DMA

        def call(spill, name):
            square = vmem((width, width), HALF)
            got = vmem((count * TILE, LANES), HALF)
            flat = vmem((count, ROWS * 2 * LANES), HALF)
            turned = vmem((ROWS * 2 * LANES, count), HALF)
            return pl.pallas_call(
                functools.partial(kernel, count_pair // 2, count_virt, spill),
                out_shape=jax.ShapeDtypeStruct((1, count), FULL),
                in_specs=[pl.BlockSpec(memory_space=pltpu.HBM)] * 8,
                out_specs=pl.BlockSpec(memory_space=vmem),
                scratch_shapes=[square] * 10
                + [vmem((spill * TILE, width), HALF)]
                + [got] * 4
                + [flat] * 3
                + [turned] * 2
                + [
                    vmem((count, count), FULL),
                    vmem((count // LANES, count, LANES), FULL),
                    vmem((count // LANES, count, LANES), FULL),
                    vmem((count // LANES, count_virt, LANES), FULL),
                    vmem((count_virt, count // LANES, count_virt, LANES), FULL),
                    smem(occ.shape, occ.dtype),
                    smem(orbitals.shape, orbitals.dtype),
                    smem(ospin.shape, ospin.dtype),
                    vmem((width // LANES, LANES), vspin.dtype),
                    vmem((1, LANES), FULL),
                    vmem((count_pair, 1, LANES), FULL),
                    vmem((1, LANES), FULL),
                    vmem((count_virt, 1, LANES), FULL),
                    vmem((count, LANES), FULL),
                    dma((8,)),
                    dma((4,)),
                    dma((4,)),
                    dma((3 + count_virt,)),
                    dma((4,)),
                    dma((4,)),
                ],
                compiler_params=pltpu.CompilerParams(
                    has_side_effects=True, vmem_limit_bytes=60 * 2**20
                ),
                name=name,
            )

        arrays = (
            amps.reshape(width, width),
            two.reshape(width, width),
            omega.reshape(width, width),
            dipole,
            occ,
            orbitals,
            ospin,
            vspin.reshape(width // LANES, LANES),
        )
        ones = jnp.sum(vspin)
        reach = width // 2 + NARROW * ROWS
        return lax.cond(
            jnp.logical_and(ones <= reach, width - ones <= reach),
            call(NARROW, "folded_gram"),
            call(width // TILE, "whole_gram"),
            *arrays,
        )

    rows = P(("pair", "virt"))
    return jax.shard_map(
        on_device,
        mesh=mesh,
        in_specs=(rows, rows, rows, P(), P(), rows, P(), P()),
        out_specs=P(("pair", "virt"), None),
        check_vma=False,
    )
```

time: 226 us -> 191 us (0.85)
  Pallas kernels: 220 us -> 188 us
  local copies, waits for them, and re-layouts: 6.4 us -> 0.56 us
    pallas_call x1, Pallas kernels: 220 us -> 188 us  [on_device(): lax.cond(jnp.logical_and(ones <= reach, width - ones <= reach), call(NARR...]
    unnamed x13 -> x1, local copies, waits for them, and re-layouts: 6.4 us -> 0.56 us
where the time goes in v2:
time: 191 us
  Pallas kernels  188 us (98%)
    pallas_call x1, Pallas kernels, on_device(): lax.cond(jnp.logical_and(ones <= reach, width - ones <= reach), call(NARR...  188 us

profile of v2, /device:TPU:1, one launch (start us, length us, event | category | flops | bytes accessed | tf_op | source)
XLA Modules:
  0.0 190.8 jit_solution(17072381731597150776)
XLA Ops:
  0.0 1.3 reduce_sum.9
  2.6 187.6 %conditional.1 = (f32[1,256]{1,0:T(1,128)S(1)}) conditional(s32[]{:T(128)} %convert_element_type.3, (bf16[1,1024,1024]{2,1,0:T(8,128)(2,1)}, bf16[1,1024,1024]{2,1,0:T(8,128)(2,1)}, bf16[1,1024,1024]{2,1,0:T(8,128)(2,1)}, bf16[1024,1024]{1,0:T(8,128)(2,1)}, f32[120]{0:T(128)}, /*index=5*/s32[1,2]{1,0:T(1,128)}, s32[120]{0:T(128)}, ...), branch_computations={%region_1.0_spmd, %region_2.0_spmd} | conditional | bytes 8 | solution.py:540
  2.6 187.6 %folded_gram.1 = f32[1,256]{1,0:T(1,128)S(1)} custom-call(bf16[1024,1024]{1,0:T(8,128)(2,1)} %bitcast.9, bf16[1024,1024]{1,0:T(8,128)(2,1)} %bitcast.11, bf16[1024,1024]{1,0:T(8,128)(2,1)} %bitcast.13, bf16[1024,1024]{1,0:T(8,128)(2,1)} %get-tuple-element.80.dipole_hbm, f32[120]{0:T(128)} %get-tuple-element.82.occ_hbm, s32[1,2]{1,0:T(1,128)} %get-tuple-element.84.orb_hbm, ...), custom_call_target="tpu_custom_call" | custom-call | tf_op jit(solution)/shard_map/cond/branch_1_fun/folded_gram/pallas_call | solution.py:540
  190.2 0.6 copy.28

commit v3 on v2

v3 whole, which is shorter than its diff:
```python
import functools

import jax
import jax.numpy as jnp
from jax import lax
from jax.experimental import pallas as pl
from jax.experimental.pallas import tpu as pltpu
from jax.sharding import PartitionSpec as P

MESH = pl.DeviceIdType.MESH
HALF, FULL = jnp.bfloat16, jnp.float32
ROWS, LANES = 16, 128
TILE = 2 * ROWS
BLOCK = 128
GROUP = 16
NARROW = 4
LAST = (((1,), (1,)), ((), ()))


def kernel(
    rings,
    count_virt,
    spill,
    amps_hbm,
    two_hbm,
    omega_hbm,
    dipole_hbm,
    occ_hbm,
    orb_hbm,
    ospin_hbm,
    vspin_hbm,
    out_ref,
    amps,
    dipole,
    omega,
    two,
    place,
    commuted,
    masked,
    put_omega,
    put_two,
    put_fold,
    put_spill,
    got_omega,
    got_two,
    got_fold,
    got_spill,
    left_omega,
    left_two,
    right_masked,
    right_commuted,
    turned_masked,
    turned_commuted,
    partial_sum,
    got_plane,
    slab,
    got_line,
    occ,
    orb,
    ospin,
    vspin,
    own_target,
    plane_target,
    row_target,
    line_target,
    targets,
    load_sem,
    own_sem,
    send_sem,
    recv_sem,
    stage_send,
    stage_recv,
):
    pair = lax.axis_index("pair")
    virt = lax.axis_index("virt")
    count_pair = 2 * rings
    count = count_pair * count_virt
    me = pair * count_virt + virt
    width = amps.shape[0]
    strips = width // TILE
    blocks = width // BLOCK
    per_block = strips // blocks
    middle = width // 2

    loads = [
        pltpu.make_async_copy(source, into, load_sem.at[k])
        for k, (source, into) in enumerate(
            (
                (vspin_hbm, vspin),
                (omega_hbm, omega),
                (amps_hbm, amps),
                (dipole_hbm, dipole),
                (two_hbm, two),
                (occ_hbm, occ),
                (orb_hbm, orb),
                (ospin_hbm, ospin),
            )
        )
    ]
    for load in loads:
        load.start()

    def strip_of(p, v):
        ring, core = p // 2, p % 2
        turned = (v + ring) % count_virt
        spot = (turned % 4) * 4 + core * 2 + turned // 4
        return spot * 2 + ring // 8, ring % 8

    def owner_of(strip, column):
        spot, ring = strip // 2, (strip % 2) * 8 + column
        turned = (spot % 2) * 4 + spot // 4
        return ring * 2 + (spot // 2) % 2, (turned + count_virt * 2 - ring) % count_virt

    my_strip, my_column = strip_of(pair, virt)
    my_piece = pair // (count_pair // blocks)
    my_block = my_strip // per_block
    in_piece = count // blocks
    spills = my_strip >= strips - spill

    def tile(ref, strip, column):
        row = pl.multiple_of(strip * TILE, TILE)
        col = pl.multiple_of(column * LANES, LANES)
        return ref.at[pl.ds(row, TILE), pl.ds(col, LANES)]

    def slot(ref, owner):
        return ref.at[pl.ds(pl.multiple_of(owner * TILE, TILE), TILE)]

    def push(which, source, target, strip, column, base, sem):
        p, v = owner_of(strip, column)
        mine = p * count_virt + v == me

        @pl.when(mine)
        def _():
            pltpu.make_async_copy(
                tile(source, strip - base, column), slot(target, me), own_sem.at[which]
            ).start()

        @pl.when(jnp.logical_not(mine))
        def _():
            pltpu.make_async_remote_copy(
                src_ref=tile(source, strip - base, column),
                dst_ref=slot(target, me),
                send_sem=send_sem.at[which],
                recv_sem=recv_sem.at[sem],
                device_id=(p, v),
                device_id_type=MESH,
            ).start()

    def send(which, make, source, target, work):
        @pl.loop(0, blocks)
        def _(k):
            block = lax.rem(k + my_piece, blocks)
            make(block)

            @pl.loop(0, per_block * 8)
            def _(i):
                j = lax.rem(i + 2 * (pair // 2) + 4 * virt, per_block * 8)
                push(
                    which,
                    source,
                    target,
                    block * per_block + (j % 2) * 2 + (j // 2) % 2,
                    j // 4,
                    0,
                    which * blocks + my_piece,
                )

            work(k)

    def waiter(which, sem, target, copies):
        part = target.at[pl.ds(0, copies * TILE)]
        return pltpu.make_async_remote_copy(
            src_ref=part,
            dst_ref=part,
            send_sem=send_sem.at[which],
            recv_sem=recv_sem.at[sem],
            device_id=(pair, virt),
            device_id_type=MESH,
        )

    def own_arrived(which, source, target, base):
        pltpu.make_async_copy(
            tile(source, my_strip - base, my_column), slot(target, me), own_sem.at[which]
        ).wait()

    def piece_of(k):
        return lax.rem(my_block + blocks - k, blocks)

    def piece_arrived(which, source, target, piece):
        @pl.when(piece == my_piece)
        def _():
            own_arrived(which, source, target, 0)
            waiter(which, which * blocks + piece, target, in_piece - 1).wait_recv()

        @pl.when(piece != my_piece)
        def _():
            waiter(which, which * blocks + piece, target, in_piece).wait_recv()

    loads[0].wait()
    spins = vspin[...].astype(FULL)
    before = (
        lax.broadcasted_iota(jnp.int32, (BLOCK, BLOCK), 0)
        < lax.broadcasted_iota(jnp.int32, (BLOCK, BLOCK), 1)
    ).astype(FULL)
    ones_before = jnp.dot(spins, before, preferred_element_type=FULL)
    ones = jnp.zeros((1, 1), FULL)
    lane = lax.broadcasted_iota(jnp.int32, (1, BLOCK), 1)
    new_row = lax.broadcasted_iota(jnp.int32, (width, BLOCK), 0)
    for k in range(blocks):
        spin = spins[k : k + 1, :]
        up = (ones_before[k : k + 1, :] + ones).astype(jnp.int32)
        spin_up = spin.astype(jnp.int32)
        rank = jnp.where(spin_up == 1, up, lane + k * BLOCK - up)
        inside = rank < middle
        row = jnp.where(inside, rank, width - 1 - rank)
        bottom = jnp.where(inside, spin_up, 1 - spin_up)
        goal = row + (row & -ROWS) + bottom * ROWS
        place[:, k * BLOCK : (k + 1) * BLOCK] = jnp.where(new_row == goal, 1.0, 0.0).astype(HALF)
        ones += jnp.sum(spin, axis=1, keepdims=True)
    zeros = width - ones

    def permuted(block, source):
        at = pl.ds(pl.multiple_of(block * BLOCK, BLOCK), BLOCK)
        return jnp.dot(place[at, :], source[...], preferred_element_type=FULL), at

    def make_from(source, put):
        def make(block):
            moved, at = permuted(block, source)
            put[at, :] = moved.astype(HALF)

        return make

    loads[1].wait()
    send(0, make_from(omega, put_omega), put_omega, got_omega, lambda k: None)

    for load in loads[2:]:
        load.wait()
    first, second = orb[0, 0], orb[0, 1]
    shift = occ[first] + occ[second]
    target_spin = (ospin[first] + ospin[second]).astype(FULL)
    def stage(which, copies, ref):
        part = ref.at[pl.ds(0, copies)]
        return pltpu.make_async_remote_copy(
            src_ref=part,
            dst_ref=part,
            send_sem=stage_send.at[which],
            recv_sem=stage_recv.at[which],
            device_id=(pair, virt),
            device_id_type=MESH,
        )

    own_target[...] = jnp.full((1, LANES), 1.0, FULL) * target_spin
    plane_target[pair] = own_target[...]

    @pl.loop(1, count_pair)
    def _(step):
        pltpu.make_async_remote_copy(
            src_ref=own_target,
            dst_ref=plane_target.at[pair],
            send_sem=stage_send.at[0],
            recv_sem=stage_recv.at[0],
            device_id=(lax.rem(pair + step, count_pair), virt),
            device_id_type=MESH,
        ).start()

    all_spins = jnp.concatenate([spins[k : k + 1, :] for k in range(blocks)], axis=1)

    @pl.loop(0, blocks)
    def _(block):
        at = pl.ds(pl.multiple_of(block * BLOCK, BLOCK), BLOCK)
        own = vspin[pl.ds(block, 1), :].astype(FULL)
        column = jnp.broadcast_to(own, (BLOCK, BLOCK)).T[:, 0:1]
        allowed = (column + all_spins) == target_spin
        rows = amps[at, :]
        value = jnp.dot(dipole[at, :], amps[...], preferred_element_type=FULL)
        value += lax.dot_general(rows, dipole[...], LAST, preferred_element_type=FULL)
        wide = rows.astype(FULL)
        value -= shift * wide
        commuted[at, :] = jnp.where(allowed, value, 0.0).astype(HALF)
        masked[at, :] = jnp.where(allowed, wide, 0.0).astype(HALF)

    def make_fold(block):
        row = (
            (block * per_block + lax.broadcasted_iota(jnp.int32, (per_block, ROWS, 1), 0)) * ROWS
            + lax.broadcasted_iota(jnp.int32, (per_block, ROWS, 1), 1)
        ).astype(FULL)
        top_in = row < zeros[:, :, None]
        bottom_in = row < ones[:, :, None]
        kept, over = [], []
        for source in (commuted, masked):
            moved, at = permuted(block, source)
            moved = moved.reshape(per_block, 2, ROWS, width)
            top, bottom = moved[:, 0], moved[:, 1]
            kept.append(jnp.where(top_in, top, 0.0) + jnp.where(bottom_in, bottom, 0.0))
            over.append(jnp.where(top_in, 0.0, top) + jnp.where(bottom_in, 0.0, bottom))
        put_fold[at, :] = jnp.stack(kept, axis=1).reshape(BLOCK, width).astype(HALF)
        first_spill = (strips - spill) // per_block

        @pl.when(block >= first_spill)
        def _():
            to = pl.ds(pl.multiple_of((block - first_spill) * BLOCK, BLOCK), BLOCK)
            put_spill[to, :] = jnp.stack(over, axis=1).reshape(BLOCK, width).astype(HALF)

    @pl.loop(0, blocks)
    def _(block):
        make_fold(block)

    stage(0, count_pair - 1, plane_target).wait_recv()
    gathered = jnp.zeros((1, LANES), FULL)
    for p in range(count_pair):
        gathered = jnp.where(lane == p, plane_target[p], gathered)
    row_target[...] = gathered
    line_target[virt] = gathered
    for step in range(1, count_virt):
        pltpu.make_async_remote_copy(
            src_ref=row_target,
            dst_ref=line_target.at[virt],
            send_sem=stage_send.at[1],
            recv_sem=stage_recv.at[1],
            device_id=(pair, lax.rem(virt + step, count_virt)),
            device_id_type=MESH,
        ).start()
    owners = spill * 8

    @pl.loop(0, owners)
    def _(i):
        j = lax.rem(i + me, owners)
        push(
            2,
            put_spill,
            got_spill,
            strips - spill + j // 8,
            j % 8,
            strips - spill,
            2 * blocks,
        )

    size = GROUP * ROWS
    row_id = lax.broadcasted_iota(jnp.int32, (size, size), 0)
    col_id = lax.broadcasted_iota(jnp.int32, (size, size), 1)
    swap = (col_id == (row_id % GROUP) * ROWS + row_id // GROUP).astype(HALF)

    def regrouped(got, g):
        block = got[pl.ds(pl.multiple_of(g * GROUP * TILE, GROUP * TILE), GROUP * TILE), :]
        block = block.reshape(GROUP, 2, ROWS, LANES)
        wide = jnp.concatenate(
            [block[:, 0].reshape(size, LANES), block[:, 1].reshape(size, LANES)], axis=1
        )
        moved = jnp.dot(swap, wide, preferred_element_type=FULL)
        return moved.reshape(ROWS, GROUP, 2 * LANES)

    def regroup(got, into, k):
        for half in range(in_piece // GROUP):
            at = pl.ds(pl.multiple_of(k * in_piece + half * GROUP, GROUP), GROUP)
            moved = regrouped(got, piece_of(k) * (in_piece // GROUP) + half).astype(HALF)
            for r in range(ROWS):
                into[at, r * 2 * LANES : (r + 1) * 2 * LANES] = moved[r]

    def take_omega(k):
        piece_arrived(0, put_omega, got_omega, piece_of(k))
        regroup(got_omega, left_omega, k)

    send(1, lambda block: None, put_fold, got_fold, take_omega)

    stage(1, count_virt - 1, line_target).wait_recv()
    for v in range(count_virt):
        column = jnp.broadcast_to(line_target[v], (LANES, LANES)).T
        targets[pl.ds(v, count_pair, stride=count_virt), :] = column[0:count_pair]
    my_spins = vspin[pl.ds(my_column, 1), :].astype(FULL)

    @pl.when(spills)
    def _():
        own_arrived(2, put_spill, got_spill, strips - spill)
        waiter(2, 2 * blocks, got_spill, count - 1).wait_recv()

    def unfold(g, with_spill):
        at = pl.ds(pl.multiple_of(g * GROUP, GROUP), GROUP)
        target = targets[at, :]
        top = (target == my_spins)[None]
        bottom = (target == my_spins + 1.0)[None]
        main = regrouped(got_fold, g)
        over = regrouped(got_spill, g) if with_spill else None
        for c, into in enumerate((right_commuted, right_masked)):
            half = main[:, :, c * LANES : (c + 1) * LANES]
            rest = over[:, :, c * LANES : (c + 1) * LANES] if with_spill else 0.0
            upper = jnp.where(top, half, jnp.where(bottom, rest, 0.0)).astype(HALF)
            lower = jnp.where(bottom, half, jnp.where(top, rest, 0.0)).astype(HALF)
            for r in range(ROWS):
                into[at, 2 * r * LANES : (2 * r + 1) * LANES] = upper[r]
                into[at, (2 * r + 1) * LANES : (2 * r + 2) * LANES] = lower[r]

    def take_fold(k):
        piece = piece_of(k)
        piece_arrived(1, put_fold, got_fold, piece)
        first_group = piece * (in_piece // GROUP)

        @pl.when(spills)
        def _():
            for half in range(in_piece // GROUP):
                unfold(first_group + half, True)

        @pl.when(jnp.logical_not(spills))
        def _():
            for half in range(in_piece // GROUP):
                unfold(first_group + half, False)

    send(3, make_from(two, put_two), put_two, got_two, take_fold)

    @pl.loop(0, ROWS)
    def _(r):
        at = pl.ds(pl.multiple_of(r * 2 * LANES, 2 * LANES), 2 * LANES)
        for flat, turned in ((right_commuted, turned_commuted), (right_masked, turned_masked)):
            turned[at, :] = flat[:, at].T

    partial_sum[...] = jnp.dot(left_omega[...], turned_masked[...], preferred_element_type=FULL)

    pairs_in_piece = count_pair // blocks

    def rows_of(ref, owner):
        return ref.at[pl.ds(pl.multiple_of(owner * count_virt, count_virt), count_virt)]

    def give(k, u):
        to_pair = piece_of(k) * pairs_in_piece + u
        source = rows_of(partial_sum, k * pairs_in_piece + u)

        @pl.when(to_pair == pair)
        def _():
            rows_of(got_plane, pair)[...] = source[...]

        @pl.when(to_pair != pair)
        def _():
            pltpu.make_async_remote_copy(
                src_ref=source,
                dst_ref=rows_of(got_plane, pair),
                send_sem=stage_send.at[2],
                recv_sem=stage_recv.at[2],
                device_id=(to_pair, virt),
                device_id_type=MESH,
            ).start()

    for start, stop in ((0, blocks // 2), (blocks // 2, blocks - 1), (blocks - 1, blocks)):

        @pl.loop(start, stop)
        def _(k):
            piece_arrived(3, put_two, got_two, piece_of(k))
            regroup(got_two, left_two, k)

        at = slice(start * in_piece, stop * in_piece)
        partial_sum[at, :] = (
            partial_sum[at, :]
            + jnp.dot(left_two[at, :], turned_commuted[...], preferred_element_type=FULL)
        ) * (1.0 / width)
        for k in range(start, stop):
            for u in range(pairs_in_piece):
                give(k, u)

    plane = stage(2, (count_pair - 1) * count_virt, got_plane)
    plane.wait_recv()
    summed = jnp.sum(got_plane[...].reshape(count_pair, count_virt, count), axis=0)
    for v in range(count_virt):
        slab[v] = summed[v : v + 1, :]

    for step in range(1, count_virt):
        pltpu.make_async_remote_copy(
            src_ref=slab.at[lax.rem(virt + step, count_virt)],
            dst_ref=got_line.at[virt],
            send_sem=stage_send.at[3],
            recv_sem=stage_recv.at[3],
            device_id=(pair, lax.rem(virt + step, count_virt)),
            device_id_type=MESH,
        ).start()
    got_line[virt] = slab[virt]
    line = stage(3, count_virt - 1, got_line)
    line.wait_recv()
    total = got_line[0]
    for v in range(1, count_virt):
        total += got_line[v]
    out_ref[...] = total
    for which, target in ((0, got_omega), (1, got_fold), (3, got_two)):
        waiter(which, which * blocks, target, count - 1).wait_send()

    @pl.when(spills)
    def _():
        waiter(2, 2 * blocks, got_spill, owners - 1).wait_send()

    @pl.when(jnp.logical_not(spills))
    def _():
        waiter(2, 2 * blocks, got_spill, owners).wait_send()

    stage(0, count_pair - 1, plane_target).wait_send()
    stage(1, count_virt - 1, line_target).wait_send()
    plane.wait_send()
    line.wait_send()


def solution(mesh):
    count_pair, count_virt = mesh.shape["pair"], mesh.shape["virt"]
    count = count_pair * count_virt

    def on_device(amps, two, omega, dipole, occ, orbitals, ospin, vspin):
        width = dipole.shape[0]
        vmem, smem, dma = pltpu.VMEM, pltpu.SMEM, pltpu.SemaphoreType.DMA

        def call(spill, name):
            square = vmem((width, width), HALF)
            got = vmem((count * TILE, LANES), HALF)
            flat = vmem((count, ROWS * 2 * LANES), HALF)
            turned = vmem((ROWS * 2 * LANES, count), HALF)
            return pl.pallas_call(
                functools.partial(kernel, count_pair // 2, count_virt, spill),
                out_shape=jax.ShapeDtypeStruct((1, count), FULL),
                in_specs=[pl.BlockSpec(memory_space=pltpu.HBM)] * 8,
                out_specs=pl.BlockSpec(memory_space=vmem),
                scratch_shapes=[square] * 10
                + [vmem((spill * TILE, width), HALF)]
                + [got] * 4
                + [flat] * 4
                + [turned] * 2
                + [
                    vmem((count, count), FULL),
                    vmem((count, count), FULL),
                    vmem((count_virt, 1, count), FULL),
                    vmem((count_virt, 1, count), FULL),
                    smem(occ.shape, occ.dtype),
                    smem(orbitals.shape, orbitals.dtype),
                    smem(ospin.shape, ospin.dtype),
                    vmem((width // LANES, LANES), vspin.dtype),
                    vmem((1, LANES), FULL),
                    vmem((count_pair, 1, LANES), FULL),
                    vmem((1, LANES), FULL),
                    vmem((count_virt, 1, LANES), FULL),
                    vmem((count, LANES), FULL),
                    dma((8,)),
                    dma((4,)),
                    dma((4,)),
                    dma((4 * width // BLOCK,)),
                    dma((4,)),
                    dma((4,)),
                ],
                compiler_params=pltpu.CompilerParams(
                    has_side_effects=True, vmem_limit_bytes=60 * 2**20
                ),
                name=name,
            )

        arrays = (
            amps.reshape(width, width),
            two.reshape(width, width),
            omega.reshape(width, width),
            dipole,
            occ,
            orbitals,
            ospin,
            vspin.reshape(width // LANES, LANES),
        )
        ones = jnp.sum(vspin)
        reach = width // 2 + NARROW * ROWS
        return lax.cond(
            jnp.logical_and(ones <= reach, width - ones <= reach),
            call(NARROW, "folded_gram"),
            call(width // TILE, "whole_gram"),
            *arrays,
        )

    rows = P(("pair", "virt"))
    return jax.shard_map(
        on_device,
        mesh=mesh,
        in_specs=(rows, rows, rows, P(), P(), rows, P(), P()),
        out_specs=P(("pair", "virt"), None),
        check_vma=False,
    )
```

time: 191 us -> 178 us (0.932)
  Pallas kernels: 188 us -> 174 us
    pallas_call x1, Pallas kernels: 188 us -> 174 us  [on_device(): lax.cond(jnp.logical_and(ones <= reach, width - ones <= reach), call(NARR...]
where the time goes in v3:
time: 178 us
  Pallas kernels  174 us (98%)
    pallas_call x1, Pallas kernels, on_device(): lax.cond(jnp.logical_and(ones <= reach, width - ones <= reach), call(NARR...  174 us

profile of v3, /device:TPU:1, one launch (start us, length us, event | category | flops | bytes accessed | tf_op | source)
XLA Modules:
  0.0 177.6 jit_solution(17692804538969673763)
XLA Ops:
  0.0 1.3 reduce_sum.9
  2.6 174.4 %conditional.1 = (f32[1,256]{1,0:T(1,128)S(1)}) conditional(s32[]{:T(128)} %convert_element_type.3, (bf16[1,1024,1024]{2,1,0:T(8,128)(2,1)}, bf16[1,1024,1024]{2,1,0:T(8,128)(2,1)}, bf16[1,1024,1024]{2,1,0:T(8,128)(2,1)}, bf16[1024,1024]{1,0:T(8,128)(2,1)}, f32[120]{0:T(128)}, /*index=5*/s32[1,2]{1,0:T(1,128)}, s32[120]{0:T(128)}, ...), branch_computations={%region_1.0_spmd, %region_2.0_spmd} | conditional | bytes 8 | solution.py:558
  2.6 174.1 %folded_gram.1 = f32[1,256]{1,0:T(1,128)S(1)} custom-call(bf16[1024,1024]{1,0:T(8,128)(2,1)} %bitcast.9, bf16[1024,1024]{1,0:T(8,128)(2,1)} %bitcast.11, bf16[1024,1024]{1,0:T(8,128)(2,1)} %bitcast.13, bf16[1024,1024]{1,0:T(8,128)(2,1)} %get-tuple-element.80.dipole_hbm, f32[120]{0:T(128)} %get-tuple-element.82.occ_hbm, s32[1,2]{1,0:T(1,128)} %get-tuple-element.84.orb_hbm, ...), custom_call_target="tpu_custom_call" | custom-call | tf_op jit(solution)/shard_map/cond/branch_1_fun/folded_gram/pallas_call | solution.py:558
  177.0 0.6 copy.28

commit v4 on v3

--- a/solution.py
+++ b/solution.py
@@ -30,6 +30,7 @@
     ospin_hbm,
     vspin_hbm,
     out_ref,
+    flag_ref,
     amps,
     dipole,
     omega,
@@ -101,19 +102,22 @@
         load.start()
 
     def strip_of(p, v):
-        ring, core = p // 2, p % 2
-        turned = (v + ring) % count_virt
-        spot = (turned % 4) * 4 + core * 2 + turned // 4
-        return spot * 2 + ring // 8, ring % 8
+        ring, core = lax.div(p, 2), lax.rem(p, 2)
+        turned = lax.rem(v + ring, count_virt)
+        spot = lax.rem(turned, 4) * 4 + core * 2 + lax.div(turned, 4)
+        return spot * 2 + lax.div(ring, 8), lax.rem(ring, 8)
 
     def owner_of(strip, column):
-        spot, ring = strip // 2, (strip % 2) * 8 + column
-        turned = (spot % 2) * 4 + spot // 4
-        return ring * 2 + (spot // 2) % 2, (turned + count_virt * 2 - ring) % count_virt
+        spot, ring = lax.div(strip, 2), lax.rem(strip, 2) * 8 + column
+        turned = lax.rem(spot, 2) * 4 + lax.div(spot, 4)
+        return (
+            ring * 2 + lax.rem(lax.div(spot, 2), 2),
+            lax.rem(turned + count_virt * 2 - ring, count_virt),
+        )
 
     my_strip, my_column = strip_of(pair, virt)
-    my_piece = pair // (count_pair // blocks)
-    my_block = my_strip // per_block
+    my_piece = lax.div(pair, count_pair // blocks)
+    my_block = lax.div(my_strip, per_block)
     in_piece = count // blocks
     spills = my_strip >= strips - spill
 
@@ -146,6 +150,8 @@
                 device_id_type=MESH,
             ).start()
 
+    turn = lax.div(pair, 2) * 2 + virt * 4
+
     def send(which, make, source, target, work):
         @pl.loop(0, blocks)
         def _(k):
@@ -154,13 +160,13 @@
 
             @pl.loop(0, per_block * 8)
             def _(i):
-                j = lax.rem(i + 2 * (pair // 2) + 4 * virt, per_block * 8)
+                j = lax.rem(i + turn, per_block * 8)
                 push(
                     which,
                     source,
                     target,
-                    block * per_block + (j % 2) * 2 + (j // 2) % 2,
-                    j // 4,
+                    block * per_block + lax.rem(j, 4),
+                    lax.div(j, 4),
                     0,
                     which * blocks + my_piece,
                 )
@@ -205,7 +211,7 @@
     ones_before = jnp.dot(spins, before, preferred_element_type=FULL)
     ones = jnp.zeros((1, 1), FULL)
     lane = lax.broadcasted_iota(jnp.int32, (1, BLOCK), 1)
-    new_row = lax.broadcasted_iota(jnp.int32, (width, BLOCK), 0)
+    goals = []
     for k in range(blocks):
         spin = spins[k : k + 1, :]
         up = (ones_before[k : k + 1, :] + ones).astype(jnp.int32)
@@ -214,10 +220,20 @@
         inside = rank < middle
         row = jnp.where(inside, rank, width - 1 - rank)
         bottom = jnp.where(inside, spin_up, 1 - spin_up)
-        goal = row + (row & -ROWS) + bottom * ROWS
-        place[:, k * BLOCK : (k + 1) * BLOCK] = jnp.where(new_row == goal, 1.0, 0.0).astype(HALF)
+        goals.append(row + (row & -ROWS) + bottom * ROWS)
         ones += jnp.sum(spin, axis=1, keepdims=True)
     zeros = width - ones
+    reach = middle + spill * ROWS
+    most = jnp.max(jnp.maximum(ones, zeros))
+    flag_ref[0, 0] = (most > reach).astype(jnp.int32)
+
+    def make_place(block):
+        at = pl.ds(pl.multiple_of(block * BLOCK, BLOCK), BLOCK)
+        new_row = lax.broadcasted_iota(jnp.int32, (BLOCK, BLOCK), 0) + block * BLOCK
+        for k in range(blocks):
+            place[at, k * BLOCK : (k + 1) * BLOCK] = jnp.where(
+                new_row == goals[k], 1.0, 0.0
+            ).astype(HALF)
 
     def permuted(block, source):
         at = pl.ds(pl.multiple_of(block * BLOCK, BLOCK), BLOCK)
@@ -230,8 +246,14 @@
 
         return make
 
+    make_omega = make_from(omega, put_omega)
+
+    def place_and_make(block):
+        make_place(block)
+        make_omega(block)
+
     loads[1].wait()
-    send(0, make_from(omega, put_omega), put_omega, got_omega, lambda k: None)
+    send(0, place_and_make, put_omega, got_omega, lambda k: None)
 
     for load in loads[2:]:
         load.wait()
@@ -329,8 +351,8 @@
             2,
             put_spill,
             got_spill,
-            strips - spill + j // 8,
-            j % 8,
+            strips - spill + lax.div(j, 8),
+            lax.rem(j, 8),
             strips - spill,
             2 * blocks,
         )
@@ -508,9 +530,12 @@
             turned = vmem((ROWS * 2 * LANES, count), HALF)
             return pl.pallas_call(
                 functools.partial(kernel, count_pair // 2, count_virt, spill),
-                out_shape=jax.ShapeDtypeStruct((1, count), FULL),
+                out_shape=(
+                    jax.ShapeDtypeStruct((1, count), FULL),
+                    jax.ShapeDtypeStruct((1, 1), jnp.int32),
+                ),
                 in_specs=[pl.BlockSpec(memory_space=pltpu.HBM)] * 8,
-                out_specs=pl.BlockSpec(memory_space=vmem),
+                out_specs=(pl.BlockSpec(memory_space=vmem), pl.BlockSpec(memory_space=smem)),
                 scratch_shapes=[square] * 10
                 + [vmem((spill * TILE, width), HALF)]
                 + [got] * 4
@@ -553,13 +578,9 @@
             ospin,
             vspin.reshape(width // LANES, LANES),
         )
-        ones = jnp.sum(vspin)
-        reach = width // 2 + NARROW * ROWS
+        gram, over = call(NARROW, "folded_gram")(*arrays)
         return lax.cond(
-            jnp.logical_and(ones <= reach, width - ones <= reach),
-            call(NARROW, "folded_gram"),
-            call(width // TILE, "whole_gram"),
-            *arrays,
+            over[0, 0] > 0, lambda _: call(width // TILE, "whole_gram")(*arrays)[0], lambda g: g, gram
         )
 
     rows = P(("pair", "virt"))

time: 178 us -> 176 us (0.989)
  no operation moved by 1% of the time
where the time goes in v4:
time: 176 us
  Pallas kernels  174 us (99%)
    pallas_call x1, Pallas kernels, on_device(): gram, over = call(NARROW, 'folded_gram')(*arrays)  174 us

profile of v4, /device:TPU:1, one launch (start us, length us, event | category | flops | bytes accessed | tf_op | source)
XLA Modules:
  0.0 175.6 jit_solution(21701488168112468)
XLA Ops:
  0.0 0.0 copy-start
  0.0 0.0 copy-start.1
  0.0 0.0 copy-start.2
  0.0 0.0 copy-start.3
  0.0 0.0 copy-start.4
  0.0 174.2 %folded_gram.1 = (f32[1,256]{1,0:T(1,128)S(1)}, s32[1,1]{1,0:T(1,128)}) custom-call(bf16[1024,1024]{1,0:T(8,128)(2,1)} %bitcast.5, bf16[1024,1024]{1,0:T(8,128)(2,1)} %bitcast.7, bf16[1024,1024]{1,0:T(8,128)(2,1)} %bitcast.9, bf16[1024,1024]{1,0:T(8,128)(2,1)} %dipole_hbm.1, f32[120]{0:T(128)} %occ_hbm.1, s32[1,2]{1,0:T(1,128)} %orb_hbm.1, s32[120]{0:T(128)} %ospin_hbm.1, ...), custom_call_target="tpu_custom_call" | custom-call | tf_op jit(solution)/shard_map/folded_gram/pallas_call | solution.py:581
  175.0 0.0 copy-done
  175.0 0.0 copy-done.1
  175.0 0.0 copy-done.2
  175.0 0.0 copy-done.3
  175.0 0.0 copy-done.4
  175.0 0.6 copy.14
  (1 shorter events, 0.0 us)
Async XLA Ops:
  0.0 175.0 %copy-start = (bf16[1,1024,1024]{2,1,0:T(8,128)(2,1)S(1)}, bf16[1,1024,1024]{2,1,0:T(8,128)(2,1)}, u32[]{:S(2)}) copy-start(bf16[1,1024,1024]{2,1,0:T(8,128)(2,1)} %param.10) | copy-start | bytes 6291460
  0.0 175.0 %copy-start.1 = (s32[1024]{0:T(1024)S(1)}, s32[1024]{0:T(1024)}, u32[]{:S(2)}) copy-start(s32[1024]{0:T(1024)} %param.17) | copy-start | bytes 12292
  0.0 175.0 %copy-start.2 = (f32[120]{0:T(128)S(1)}, f32[120]{0:T(128)}, u32[]{:S(2)}) copy-start(f32[120]{0:T(128)} %occ_hbm.1) | copy-start | bytes 1444
  0.0 175.0 %copy-start.3 = (s32[1,2]{1,0:T(1,128)S(1)}, s32[1,2]{1,0:T(1,128)}, u32[]{:S(2)}) copy-start(s32[1,2]{1,0:T(1,128)} %orb_hbm.1) | copy-start | bytes 28
  0.0 175.0 %copy-start.4 = (s32[120]{0:T(128)S(1)}, s32[120]{0:T(128)}, u32[]{:S(2)}) copy-start(s32[120]{0:T(128)} %ospin_hbm.1) | copy-start | bytes 1444

commit v5 on v4

--- a/solution.py
+++ b/solution.py
@@ -56,6 +56,8 @@
     got_plane,
     slab,
     got_line,
+    put_rows,
+    got_rows,
     occ,
     orb,
     ospin,
@@ -202,6 +204,7 @@
         def _():
             waiter(which, which * blocks + piece, target, in_piece).wait_recv()
 
+    got_plane[...] = jnp.zeros_like(got_plane)
     loads[0].wait()
     spins = vspin[...].astype(FULL)
     before = (
@@ -460,7 +463,8 @@
                 device_id_type=MESH,
             ).start()
 
-    for start, stop in ((0, blocks // 2), (blocks // 2, blocks - 1), (blocks - 1, blocks)):
+    last = blocks - 1
+    for start, stop in ((0, blocks // 2), (blocks // 2, last), (last, blocks)):
 
         @pl.loop(start, stop)
         def _(k):
@@ -472,12 +476,51 @@
             partial_sum[at, :]
             + jnp.dot(left_two[at, :], turned_commuted[...], preferred_element_type=FULL)
         ) * (1.0 / width)
-        for k in range(start, stop):
-            for u in range(pairs_in_piece):
-                give(k, u)
-
-    plane = stage(2, (count_pair - 1) * count_virt, got_plane)
-    plane.wait_recv()
+        if start < last:
+            for k in range(start, stop):
+                for u in range(pairs_in_piece):
+                    give(k, u)
+        else:
+            for i in range(in_piece):
+                put_rows[i] = partial_sum[start * in_piece + i : start * in_piece + i + 1, :]
+
+    my_row = lax.rem(my_strip, per_block) * 8 + my_column
+    first_pair = piece_of(last) * pairs_in_piece
+
+    @pl.loop(0, in_piece)
+    def _(step):
+        i = lax.rem(step + my_row, in_piece)
+        to_pair, to_virt = first_pair + lax.div(i, count_virt), lax.rem(i, count_virt)
+        mine = to_pair * count_virt + to_virt == me
+
+        @pl.when(mine)
+        def _():
+            got_rows[my_row] = put_rows[i]
+
+        @pl.when(jnp.logical_not(mine))
+        def _():
+            pltpu.make_async_remote_copy(
+                src_ref=put_rows.at[i],
+                dst_ref=got_rows.at[my_row],
+                send_sem=stage_send.at[4],
+                recv_sem=stage_recv.at[4],
+                device_id=(to_pair, to_virt),
+                device_id_type=MESH,
+            ).start()
+
+    straight = piece_of(last) == my_piece
+    strips_sent = (count_pair - pairs_in_piece) * count_virt
+
+    def for_each(work):
+        @pl.when(straight)
+        def _():
+            work(strips_sent, in_piece - 1)
+
+        @pl.when(jnp.logical_not(straight))
+        def _():
+            work(strips_sent - count_virt, in_piece)
+
+    for_each(lambda strips_in, _: stage(2, strips_in, got_plane).wait_recv())
     summed = jnp.sum(got_plane[...].reshape(count_pair, count_virt, count), axis=0)
     for v in range(count_virt):
         slab[v] = summed[v : v + 1, :]
@@ -494,7 +537,8 @@
     got_line[virt] = slab[virt]
     line = stage(3, count_virt - 1, got_line)
     line.wait_recv()
-    total = got_line[0]
+    for_each(lambda _, rows_in: stage(4, rows_in, got_rows).wait_recv())
+    total = jnp.sum(got_rows[...], axis=0) + got_line[0]
     for v in range(1, count_virt):
         total += got_line[v]
     out_ref[...] = total
@@ -511,8 +555,13 @@
 
     stage(0, count_pair - 1, plane_target).wait_send()
     stage(1, count_virt - 1, line_target).wait_send()
-    plane.wait_send()
     line.wait_send()
+
+    def sent(strips_out, rows_out):
+        stage(2, strips_out, got_plane).wait_send()
+        stage(4, rows_out, got_rows).wait_send()
+
+    for_each(sent)
 
 
 def solution(mesh):
@@ -546,6 +595,8 @@
                     vmem((count, count), FULL),
                     vmem((count_virt, 1, count), FULL),
                     vmem((count_virt, 1, count), FULL),
+                    vmem((count * BLOCK // width, 1, count), FULL),
+                    vmem((count * BLOCK // width, 1, count), FULL),
                     smem(occ.shape, occ.dtype),
                     smem(orbitals.shape, orbitals.dtype),
                     smem(ospin.shape, ospin.dtype),
@@ -559,8 +610,8 @@
                     dma((4,)),
                     dma((4,)),
                     dma((4 * width // BLOCK,)),
-                    dma((4,)),
-                    dma((4,)),
+                    dma((5,)),
+                    dma((5,)),
                 ],
                 compiler_params=pltpu.CompilerParams(
                     has_side_effects=True, vmem_limit_bytes=60 * 2**20

time: 176 us -> 175 us (level)
  no operation moved by 1% of the time
where the time goes in v5:
time: 175 us; the launch traced here: 174 us
  Pallas kernels  173 us (99%)
    pallas_call x1, Pallas kernels, on_device(): gram, over = call(NARROW, 'folded_gram')(*arrays)  173 us

profile of v5, /device:TPU:1, one launch (start us, length us, event | category | flops | bytes accessed | tf_op | source)
XLA Modules:
  0.0 174.4 jit_solution(5586543204157939171)
XLA Ops:
  0.0 0.0 copy-start
  0.0 0.0 copy-start.1
  0.0 0.0 copy-start.2
  0.0 0.0 copy-start.3
  0.0 0.0 copy-start.4
  0.0 173.1 %folded_gram.1 = (f32[1,256]{1,0:T(1,128)S(1)}, s32[1,1]{1,0:T(1,128)}) custom-call(bf16[1024,1024]{1,0:T(8,128)(2,1)} %bitcast.5, bf16[1024,1024]{1,0:T(8,128)(2,1)} %bitcast.7, bf16[1024,1024]{1,0:T(8,128)(2,1)} %bitcast.9, bf16[1024,1024]{1,0:T(8,128)(2,1)} %dipole_hbm.1, f32[120]{0:T(128)} %occ_hbm.1, s32[1,2]{1,0:T(1,128)} %orb_hbm.1, s32[120]{0:T(128)} %ospin_hbm.1, ...), custom_call_target="tpu_custom_call" | custom-call | tf_op jit(solution)/shard_map/folded_gram/pallas_call | solution.py:632
  173.8 0.0 copy-done
  173.8 0.0 copy-done.1
  173.8 0.0 copy-done.2
  173.8 0.0 copy-done.3
  173.8 0.0 copy-done.4
  173.9 0.6 copy.14
  (1 shorter events, 0.0 us)
Async XLA Ops:
  0.0 173.8 %copy-start = (bf16[1,1024,1024]{2,1,0:T(8,128)(2,1)S(1)}, bf16[1,1024,1024]{2,1,0:T(8,128)(2,1)}, u32[]{:S(2)}) copy-start(bf16[1,1024,1024]{2,1,0:T(8,128)(2,1)} %param.10) | copy-start | bytes 6291460
  0.0 173.8 %copy-start.1 = (s32[1024]{0:T(1024)S(1)}, s32[1024]{0:T(1024)}, u32[]{:S(2)}) copy-start(s32[1024]{0:T(1024)} %param.17) | copy-start | bytes 12292
  0.0 173.8 %copy-start.2 = (f32[120]{0:T(128)S(1)}, f32[120]{0:T(128)}, u32[]{:S(2)}) copy-start(f32[120]{0:T(128)} %occ_hbm.1) | copy-start | bytes 1444
  0.0 173.8 %copy-start.3 = (s32[1,2]{1,0:T(1,128)S(1)}, s32[1,2]{1,0:T(1,128)}, u32[]{:S(2)}) copy-start(s32[1,2]{1,0:T(1,128)} %orb_hbm.1) | copy-start | bytes 28
  0.0 173.8 %copy-start.4 = (s32[120]{0:T(128)S(1)}, s32[120]{0:T(128)}, u32[]{:S(2)}) copy-start(s32[120]{0:T(128)} %ospin_hbm.1) | copy-start | bytes 1444

commit v6 on v5

--- a/solution.py
+++ b/solution.py
@@ -487,7 +487,7 @@
     my_row = lax.rem(my_strip, per_block) * 8 + my_column
     first_pair = piece_of(last) * pairs_in_piece
 
-    @pl.loop(0, in_piece)
+    @pl.loop(0, in_piece, unroll=4)
     def _(step):
         i = lax.rem(step + my_row, in_piece)
         to_pair, to_virt = first_pair + lax.div(i, count_virt), lax.rem(i, count_virt)

time: 175 us -> 174 us (level)
  no operation moved by 1% of the time
where the time goes in v6:
time: 174 us
  Pallas kernels  173 us (99%)
    pallas_call x1, Pallas kernels, on_device(): gram, over = call(NARROW, 'folded_gram')(*arrays)  173 us

profile of v6, /device:TPU:1, one launch (start us, length us, event | category | flops | bytes accessed | tf_op | source)
XLA Modules:
  0.0 174.4 jit_solution(17786260136922723318)
XLA Ops:
  0.0 0.0 copy-start
  0.0 0.0 copy-start.1
  0.0 0.0 copy-start.2
  0.0 0.0 copy-start.3
  0.0 0.0 copy-start.4
  0.0 173.1 %folded_gram.1 = (f32[1,256]{1,0:T(1,128)S(1)}, s32[1,1]{1,0:T(1,128)}) custom-call(bf16[1024,1024]{1,0:T(8,128)(2,1)} %bitcast.5, bf16[1024,1024]{1,0:T(8,128)(2,1)} %bitcast.7, bf16[1024,1024]{1,0:T(8,128)(2,1)} %bitcast.9, bf16[1024,1024]{1,0:T(8,128)(2,1)} %dipole_hbm.1, f32[120]{0:T(128)} %occ_hbm.1, s32[1,2]{1,0:T(1,128)} %orb_hbm.1, s32[120]{0:T(128)} %ospin_hbm.1, ...), custom_call_target="tpu_custom_call" | custom-call | tf_op jit(solution)/shard_map/folded_gram/pallas_call | solution.py:632
  173.8 0.0 copy-done
  173.8 0.0 copy-done.1
  173.8 0.0 copy-done.2
  173.8 0.0 copy-done.3
  173.8 0.0 copy-done.4
  173.8 0.6 copy.14
  (1 shorter events, 0.0 us)
Async XLA Ops:
  0.0 173.8 %copy-start = (bf16[1,1024,1024]{2,1,0:T(8,128)(2,1)S(1)}, bf16[1,1024,1024]{2,1,0:T(8,128)(2,1)}, u32[]{:S(2)}) copy-start(bf16[1,1024,1024]{2,1,0:T(8,128)(2,1)} %param.10) | copy-start | bytes 6291460
  0.0 173.8 %copy-start.1 = (s32[1024]{0:T(1024)S(1)}, s32[1024]{0:T(1024)}, u32[]{:S(2)}) copy-start(s32[1024]{0:T(1024)} %param.17) | copy-start | bytes 12292
  0.0 173.8 %copy-start.2 = (f32[120]{0:T(128)S(1)}, f32[120]{0:T(128)}, u32[]{:S(2)}) copy-start(f32[120]{0:T(128)} %occ_hbm.1) | copy-start | bytes 1444
  0.0 173.8 %copy-start.3 = (s32[1,2]{1,0:T(1,128)S(1)}, s32[1,2]{1,0:T(1,128)}, u32[]{:S(2)}) copy-start(s32[1,2]{1,0:T(1,128)} %orb_hbm.1) | copy-start | bytes 28
  0.0 173.8 %copy-start.4 = (s32[120]{0:T(128)S(1)}, s32[120]{0:T(128)}, u32[]{:S(2)}) copy-start(s32[120]{0:T(128)} %ospin_hbm.1) | copy-start | bytes 1444
